TPU v7x, 32 devices: a whole 2x2x4 slice. The times are simulated.
32 devices in a mesh: samp: 8 (over z, x), head: 4 (over y, core).
Axes of the slice: x: 2, y: 2, z: 4, core: 2. Of those that a mesh axis runs over, the one named last changes fastest.
Arguments:
- single: bfloat16 [64, 768, 768], P('samp', 'head'), may hold values from -6 to 6
- cond: bfloat16 [64, 768, 384], P('samp', 'head'), may hold values from -6 to 6
- pair: bfloat16 [2, 768, 768, 128], P(None, 'head', 'samp'), may hold values from -6 to 6
- complex_length: int32 [2], replicated, may hold values from 384 to 768, as said below
- sample_complex: int32 [64], P('samp'), may hold values from 0 to 1
- cotangent: bfloat16 [64, 768, 768], P('samp', 'head'), may hold values from -6 to 6
- gain_one: bfloat16 [384], replicated, may hold values from 0.5 to 1.5
- w_scale_one: bfloat16 [384, 768], replicated, may hold values from -0.3125 to 0.3125
- b_scale_one: bfloat16 [768], replicated, may hold values from -3 to 3
- w_shift_one: bfloat16 [384, 768], replicated, may hold values from -0.3125 to 0.3125
- w_query: bfloat16 [768, 768], replicated, may hold values from -0.21875 to 0.21875
- b_query: bfloat16 [768], replicated, may hold values from -3 to 3
- w_key: bfloat16 [768, 768], replicated, may hold values from -0.21875 to 0.21875
- w_value: bfloat16 [768, 768], replicated, may hold values from -0.21875 to 0.21875
- w_gate: bfloat16 [768, 768], replicated, may hold values from -0.21875 to 0.21875
- w_out: bfloat16 [768, 768], replicated, may hold values from -0.875 to 0.875
- w_pair: bfloat16 [128, 16], replicated, may hold values from -0.5 to 0.5
- w_attn_cond: bfloat16 [384, 768], replicated, may hold values from -0.3125 to 0.3125
- b_attn_cond: bfloat16 [768], replicated, may hold values from -3 to 3
- gain_two: bfloat16 [384], replicated, may hold values from 0.5 to 1.5
- w_scale_two: bfloat16 [384, 768], replicated, may hold values from -0.3125 to 0.3125
- b_scale_two: bfloat16 [768], replicated, may hold values from -3 to 3
- w_shift_two: bfloat16 [384, 768], replicated, may hold values from -0.3125 to 0.3125
- w_hidden_gate: bfloat16 [768, 1536], replicated, may hold values from -0.21875 to 0.21875
- w_hidden_up: bfloat16 [768, 1536], replicated, may hold values from -0.21875 to 0.21875
- w_hidden_down: bfloat16 [1536, 768], replicated, may hold values from -0.15625 to 0.15625
- w_tr_cond: bfloat16 [384, 768], replicated, may hold values from -0.3125 to 0.3125
- b_tr_cond: bfloat16 [768], replicated, may hold values from -3 to 3
Outputs:
- block_out: bfloat16 [64, 768, 768], P('samp', 'head')
- grad_single: float32 [64, 768, 768], P('samp', 'head')
- grad_pair: float32 [2, 768, 768, 128], P(None, 'head', 'samp')
- grad_gain_one: float32 [384], replicated
- grad_w_scale_one: float32 [384, 768], P('samp', 'head')
- grad_b_scale_one: float32 [768], replicated
- grad_w_shift_one: float32 [384, 768], P('samp', 'head')
- grad_w_query: float32 [768, 768], P('samp', 'head')
- grad_b_query: float32 [768], replicated
- grad_w_key: float32 [768, 768], P('samp', 'head')
- grad_w_value: float32 [768, 768], P('samp', 'head')
- grad_w_gate: float32 [768, 768], P('samp', 'head')
- grad_w_out: float32 [768, 768], P('samp', 'head')
- grad_w_pair: float32 [128, 16], replicated
- grad_w_attn_cond: float32 [384, 768], P('samp', 'head')
- grad_b_attn_cond: float32 [768], replicated
- grad_gain_two: float32 [384], replicated
- grad_w_scale_two: float32 [384, 768], P('samp', 'head')
- grad_b_scale_two: float32 [768], replicated
- grad_w_shift_two: float32 [384, 768], P('samp', 'head')
- grad_w_hidden_gate: float32 [768, 1536], P('samp', 'head')
- grad_w_hidden_up: float32 [768, 1536], P('samp', 'head')
- grad_w_hidden_down: float32 [1536, 768], P('samp', 'head')
- grad_w_tr_cond: float32 [384, 768], P('samp', 'head')
- grad_b_tr_cond: float32 [768], replicated
Inputs may be any that keep to these rules, and one draw needn't show every extreme that they name: A sample attends to the first complex_length tokens of its complex; one complex, drawn from the seed, has more than 672.
All inputs are finite; a program needn't handle non-finite values.
Results may differ from a plain program's by a relative error of at most 0.017.
Values may be sent and summed in bfloat16 or wider, within the bound.
No kernel may reach another device: no remote copies, remote signals or barrier semaphores. Data moves between devices by JAX's collectives and lax.ppermute only.
A program may use at most 320 MiB of HBM per device.

v0:
```python
import math

import jax
import jax.numpy as jnp
from jax import lax
from jax.sharding import PartitionSpec as P

epsilon = 1e-05
fill_value = -1e30


def norm_rows(inputs):
    mean_val = jnp.mean(inputs, axis=-1, keepdims=True)
    centered = inputs - mean_val
    variance = jnp.mean(centered * centered, axis=-1, keepdims=True)
    inverse = lax.rsqrt(variance + epsilon)
    return (centered * inverse, inverse)


def norm_back(normed, inverse, upstream):
    mean_grad = jnp.mean(upstream, axis=-1, keepdims=True)
    mean_dot = jnp.mean(upstream * normed, axis=-1, keepdims=True)
    return inverse * (upstream - mean_grad - normed * mean_dot)


def project(inputs, weight):
    return jnp.dot(inputs, weight, preferred_element_type=jnp.float32)


def project_back(upstream, weight):
    return lax.dot_general(
        upstream,
        weight,
        (((upstream.ndim - 1,), (1,)), ((), ())),
        preferred_element_type=jnp.float32,
    )


def outer_total(left, right):
    left_rows = left.reshape(-1, left.shape[-1])
    right_rows = right.reshape(-1, right.shape[-1])
    return lax.dot_general(
        left_rows, right_rows, (((0,), (0,)), ((), ())), preferred_element_type=jnp.float32
    )


def row_total(upstream):
    return jnp.sum(upstream.astype(jnp.float32), axis=(0, 1))


def adaptive_forward(inputs, cond_hat, gain, w_scale, b_scale, w_shift):
    normed, inverse = norm_rows(inputs)
    cond_low = (cond_hat * gain.astype(jnp.float32)).astype(jnp.bfloat16)
    scale_gate = jax.nn.sigmoid(project(cond_low, w_scale) + b_scale.astype(jnp.float32))
    shifted = project(cond_low, w_shift)
    return (scale_gate * normed + shifted, (normed, inverse, cond_low, scale_gate))


def adaptive_backward(upstream, kept, cond_hat, w_scale, w_shift):
    normed, inverse, cond_low, scale_gate = kept
    d_scale = (upstream * normed * scale_gate * (1.0 - scale_gate)).astype(jnp.bfloat16)
    d_shift = upstream.astype(jnp.bfloat16)
    d_cond = project_back(d_scale, w_scale) + project_back(d_shift, w_shift)
    grad_gain = jnp.sum(d_cond * cond_hat, axis=(0, 1))
    grads = (
        grad_gain,
        outer_total(cond_low, d_scale),
        row_total(d_scale),
        outer_total(cond_low, d_shift),
    )
    return (norm_back(normed, inverse, upstream * scale_gate), grads)


def on_device(
    single,
    cond,
    pair,
    complex_length,
    sample_complex,
    cotangent,
    gain_one,
    w_scale_one,
    b_scale_one,
    w_shift_one,
    w_query,
    b_query,
    w_key,
    w_value,
    w_gate,
    w_out,
    w_pair,
    w_attn_cond,
    b_attn_cond,
    gain_two,
    w_scale_two,
    b_scale_two,
    w_shift_two,
    w_hidden_gate,
    w_hidden_up,
    w_hidden_down,
    w_tr_cond,
    b_tr_cond,
):
    head_count = lax.axis_size("head")
    rows_dev = single.shape[1]
    width = single.shape[2]
    seq_len = rows_dev * head_count
    heads_all = w_pair.shape[1]
    heads_dev = heads_all // head_count
    head_dim = width // heads_all
    score_scale = 1.0 / math.sqrt(head_dim)
    complexes = complex_length.shape[0]
    pair_normed, pair_inverse = norm_rows(pair.astype(jnp.float32))
    pair_low = pair_normed.astype(jnp.bfloat16)
    bias_local = jnp.einsum(
        "cijz,zh->chij", pair_low, w_pair, preferred_element_type=jnp.float32
    ).astype(jnp.bfloat16)
    bias_tall = lax.all_to_all(bias_local, "head", split_axis=1, concat_axis=2, tiled=True)
    bias_all = lax.all_gather(bias_tall, "samp", axis=3, tiled=True)
    picks = (sample_complex[:, None] == jnp.arange(complexes)[None, :]).astype(jnp.int32)
    lengths = jnp.sum(picks * complex_length[None, :], axis=1)
    key_pos = jnp.arange(seq_len)
    cond_hat, cond_inverse = norm_rows(cond.astype(jnp.float32))
    single_f = single.astype(jnp.float32)
    adapted_one, kept_one = adaptive_forward(
        single_f, cond_hat, gain_one, w_scale_one, b_scale_one, w_shift_one
    )
    adapted_one = adapted_one.astype(jnp.bfloat16)
    query_rows = (project(adapted_one, w_query) + b_query.astype(jnp.float32)).astype(jnp.bfloat16)
    key_rows = project(adapted_one, w_key).astype(jnp.bfloat16)
    value_rows = project(adapted_one, w_value).astype(jnp.bfloat16)
    gate_val = jax.nn.sigmoid(project(adapted_one, w_gate))
    query_heads, key_heads, value_heads = (
        lax.all_to_all(query_rows, "head", split_axis=2, concat_axis=1, tiled=True),
        lax.all_to_all(key_rows, "head", split_axis=2, concat_axis=1, tiled=True),
        lax.all_to_all(value_rows, "head", split_axis=2, concat_axis=1, tiled=True),
    )

    def score_block(query_one, key_one, complex_id, length_one):
        query_split = query_one.reshape(seq_len, heads_dev, head_dim)
        key_split = key_one.reshape(seq_len, heads_dev, head_dim)
        bias_one = lax.dynamic_index_in_dim(bias_all, complex_id, 0, keepdims=False)
        raw = jnp.einsum("ihd,jhd->hij", query_split, key_split, preferred_element_type=jnp.float32)
        scores = raw * score_scale + bias_one.astype(jnp.float32)
        scores = jnp.where((key_pos < length_one)[None, None, :], scores, fill_value)
        return (scores, query_split, key_split)

    def attend(items):
        query_one, key_one, value_one, complex_id, length_one = items
        scores, query_split, key_split = score_block(query_one, key_one, complex_id, length_one)
        row_max = jnp.max(scores, axis=-1, keepdims=True)
        exp_scores = jnp.exp(scores - row_max)
        totals = jnp.sum(exp_scores, axis=-1, keepdims=True)
        probs = (exp_scores / totals).astype(jnp.bfloat16)
        value_split = value_one.reshape(seq_len, heads_dev, head_dim)
        mixed = jnp.einsum("hij,jhd->ihd", probs, value_split, preferred_element_type=jnp.float32)
        mixed = mixed.reshape(seq_len, heads_dev * head_dim).astype(jnp.bfloat16)
        return (mixed, (row_max + jnp.log(totals))[..., 0])

    attended_heads, log_totals = lax.map(
        attend, (query_heads, key_heads, value_heads, sample_complex, lengths)
    )
    attended = lax.all_to_all(attended_heads, "head", split_axis=1, concat_axis=2, tiled=True)
    attended_f = attended.astype(jnp.float32)
    gated = (attended_f * gate_val).astype(jnp.bfloat16)
    attn_branch = project(gated, w_out)
    attn_cond = jax.nn.sigmoid(project(cond, w_attn_cond) + b_attn_cond.astype(jnp.float32))
    middle = single_f + attn_cond * attn_branch
    adapted_two, kept_two = adaptive_forward(
        middle, cond_hat, gain_two, w_scale_two, b_scale_two, w_shift_two
    )
    adapted_two = adapted_two.astype(jnp.bfloat16)
    hidden_gate = project(adapted_two, w_hidden_gate)
    hidden_up = project(adapted_two, w_hidden_up)
    gate_sig = jax.nn.sigmoid(hidden_gate)
    silu_val = hidden_gate * gate_sig
    hidden = (silu_val * hidden_up).astype(jnp.bfloat16)
    tr_branch = project(hidden, w_hidden_down)
    tr_cond = jax.nn.sigmoid(project(cond, w_tr_cond) + b_tr_cond.astype(jnp.float32))
    block_out = (middle + tr_cond * tr_branch).astype(jnp.bfloat16)
    upstream = cotangent.astype(jnp.float32)
    d_tr = (tr_cond * upstream).astype(jnp.bfloat16)
    d_trc = (upstream * tr_branch * tr_cond * (1.0 - tr_cond)).astype(jnp.bfloat16)
    grad_tr_cond = outer_total(cond, d_trc)
    grad_tr_bias = row_total(d_trc)
    grad_down = outer_total(hidden, d_tr)
    d_hidden = project_back(d_tr, w_hidden_down)
    d_hgate = (d_hidden * hidden_up * gate_sig * (1.0 + hidden_gate * (1.0 - gate_sig))).astype(
        jnp.bfloat16
    )
    d_hup = (d_hidden * silu_val).astype(jnp.bfloat16)
    grad_hgate = outer_total(adapted_two, d_hgate)
    grad_hup = outer_total(adapted_two, d_hup)
    d_adapted_two = project_back(d_hgate, w_hidden_gate) + project_back(d_hup, w_hidden_up)
    d_mid_norm, grads_two = adaptive_backward(
        d_adapted_two, kept_two, cond_hat, w_scale_two, w_shift_two
    )
    d_middle = upstream + d_mid_norm
    d_attn = (attn_cond * d_middle).astype(jnp.bfloat16)
    d_acond = (d_middle * attn_branch * attn_cond * (1.0 - attn_cond)).astype(jnp.bfloat16)
    grad_attn_cond = outer_total(cond, d_acond)
    grad_attn_bias = row_total(d_acond)
    grad_out = outer_total(gated, d_attn)
    d_gated = project_back(d_attn, w_out)
    d_attended = (d_gated * gate_val).astype(jnp.bfloat16)
    d_gate = (d_gated * attended_f * gate_val * (1.0 - gate_val)).astype(jnp.bfloat16)
    grad_gate = outer_total(adapted_one, d_gate)
    upstream_heads = lax.all_to_all(d_attended, "head", split_axis=2, concat_axis=1, tiled=True)

    def attend_back(bias_grad, items):
        query_one, key_one, value_one, upstream_one, log_one, complex_id, length_one = items
        scores, query_split, key_split = score_block(query_one, key_one, complex_id, length_one)
        probs = jnp.exp(scores - log_one[..., None])
        value_split = value_one.reshape(seq_len, heads_dev, head_dim)
        upstream_split = upstream_one.reshape(seq_len, heads_dev, head_dim)
        d_probs = jnp.einsum(
            "ihd,jhd->hij", upstream_split, value_split, preferred_element_type=jnp.float32
        )
        delta = jnp.sum(probs * d_probs, axis=-1, keepdims=True)
        d_scores = (probs * (d_probs - delta)).astype(jnp.bfloat16)
        d_query = (
            jnp.einsum("hij,jhd->ihd", d_scores, key_split, preferred_element_type=jnp.float32)
            * score_scale
        )
        d_key = (
            jnp.einsum("hij,ihd->jhd", d_scores, query_split, preferred_element_type=jnp.float32)
            * score_scale
        )
        d_value = jnp.einsum(
            "hij,ihd->jhd",
            probs.astype(jnp.bfloat16),
            upstream_split,
            preferred_element_type=jnp.float32,
        )
        previous = lax.dynamic_index_in_dim(bias_grad, complex_id, 0, keepdims=False)
        bias_grad = lax.dynamic_update_index_in_dim(
            bias_grad, previous + d_scores.astype(jnp.float32), complex_id, 0
        )
        flat_shape = (seq_len, heads_dev * head_dim)
        return (
            bias_grad,
            (
                d_query.reshape(flat_shape).astype(jnp.bfloat16),
                d_key.reshape(flat_shape).astype(jnp.bfloat16),
                d_value.reshape(flat_shape).astype(jnp.bfloat16),
            ),
        )

    bias_start = jnp.zeros((complexes, heads_dev, seq_len, seq_len), jnp.float32)
    bias_grad, (dquery_heads, dkey_heads, dvalue_heads) = lax.scan(
        attend_back,
        bias_start,
        (query_heads, key_heads, value_heads, upstream_heads, log_totals, sample_complex, lengths),
    )
    dquery_rows, dkey_rows, dvalue_rows = (
        lax.all_to_all(dquery_heads, "head", split_axis=1, concat_axis=2, tiled=True),
        lax.all_to_all(dkey_heads, "head", split_axis=1, concat_axis=2, tiled=True),
        lax.all_to_all(dvalue_heads, "head", split_axis=1, concat_axis=2, tiled=True),
    )
    grad_query = outer_total(adapted_one, dquery_rows)
    grad_query_bias = row_total(dquery_rows)
    grad_key = outer_total(adapted_one, dkey_rows)
    grad_value = outer_total(adapted_one, dvalue_rows)
    d_adapted_one = (
        project_back(dquery_rows, w_query)
        + project_back(dkey_rows, w_key)
        + project_back(dvalue_rows, w_value)
        + project_back(d_gate, w_gate)
    )
    d_single_norm, grads_one = adaptive_backward(
        d_adapted_one, kept_one, cond_hat, w_scale_one, w_shift_one
    )
    grad_single = d_middle + d_single_norm
    bias_summed = lax.psum_scatter(bias_grad, "samp", scatter_dimension=3, tiled=True).astype(
        jnp.bfloat16
    )
    bias_back = lax.all_to_all(bias_summed, "head", split_axis=2, concat_axis=1, tiled=True)
    grad_pair_weight = jnp.einsum(
        "cijz,chij->zh", pair_low, bias_back, preferred_element_type=jnp.float32
    )
    d_pair_norm = jnp.einsum("chij,zh->cijz", bias_back, w_pair, preferred_element_type=jnp.float32)
    grad_pair = norm_back(pair_normed, pair_inverse, d_pair_norm)
    partial_sums = (
        lax.psum_scatter(
            grads_one[1].astype(jnp.bfloat16), "head", scatter_dimension=1, tiled=True
        ).astype(jnp.float32),
        lax.psum_scatter(
            grads_one[3].astype(jnp.bfloat16), "head", scatter_dimension=1, tiled=True
        ).astype(jnp.float32),
        lax.psum_scatter(
            grad_query.astype(jnp.bfloat16), "head", scatter_dimension=1, tiled=True
        ).astype(jnp.float32),
        lax.psum_scatter(
            grad_key.astype(jnp.bfloat16), "head", scatter_dimension=1, tiled=True
        ).astype(jnp.float32),
        lax.psum_scatter(
            grad_value.astype(jnp.bfloat16), "head", scatter_dimension=1, tiled=True
        ).astype(jnp.float32),
        lax.psum_scatter(
            grad_gate.astype(jnp.bfloat16), "head", scatter_dimension=1, tiled=True
        ).astype(jnp.float32),
        lax.psum_scatter(
            grad_out.astype(jnp.bfloat16), "head", scatter_dimension=1, tiled=True
        ).astype(jnp.float32),
        lax.psum_scatter(
            grad_attn_cond.astype(jnp.bfloat16), "head", scatter_dimension=1, tiled=True
        ).astype(jnp.float32),
        lax.psum_scatter(
            grads_two[1].astype(jnp.bfloat16), "head", scatter_dimension=1, tiled=True
        ).astype(jnp.float32),
        lax.psum_scatter(
            grads_two[3].astype(jnp.bfloat16), "head", scatter_dimension=1, tiled=True
        ).astype(jnp.float32),
        lax.psum_scatter(
            grad_hgate.astype(jnp.bfloat16), "head", scatter_dimension=1, tiled=True
        ).astype(jnp.float32),
        lax.psum_scatter(
            grad_hup.astype(jnp.bfloat16), "head", scatter_dimension=1, tiled=True
        ).astype(jnp.float32),
        lax.psum_scatter(
            grad_down.astype(jnp.bfloat16), "head", scatter_dimension=1, tiled=True
        ).astype(jnp.float32),
        lax.psum_scatter(
            grad_tr_cond.astype(jnp.bfloat16), "head", scatter_dimension=1, tiled=True
        ).astype(jnp.float32),
    )
    summed = (
        lax.psum_scatter(partial_sums[0], "samp", scatter_dimension=0, tiled=True),
        lax.psum_scatter(partial_sums[1], "samp", scatter_dimension=0, tiled=True),
        lax.psum_scatter(partial_sums[2], "samp", scatter_dimension=0, tiled=True),
        lax.psum_scatter(partial_sums[3], "samp", scatter_dimension=0, tiled=True),
        lax.psum_scatter(partial_sums[4], "samp", scatter_dimension=0, tiled=True),
        lax.psum_scatter(partial_sums[5], "samp", scatter_dimension=0, tiled=True),
        lax.psum_scatter(partial_sums[6], "samp", scatter_dimension=0, tiled=True),
        lax.psum_scatter(partial_sums[7], "samp", scatter_dimension=0, tiled=True),
        lax.psum_scatter(partial_sums[8], "samp", scatter_dimension=0, tiled=True),
        lax.psum_scatter(partial_sums[9], "samp", scatter_dimension=0, tiled=True),
        lax.psum_scatter(partial_sums[10], "samp", scatter_dimension=0, tiled=True),
        lax.psum_scatter(partial_sums[11], "samp", scatter_dimension=0, tiled=True),
        lax.psum_scatter(partial_sums[12], "samp", scatter_dimension=0, tiled=True),
        lax.psum_scatter(partial_sums[13], "samp", scatter_dimension=0, tiled=True),
    )
    small_sums = lax.psum(
        (
            grad_pair_weight,
            grads_one[0],
            grads_two[0],
            grads_one[2],
            grad_query_bias,
            grad_attn_bias,
            grads_two[2],
            grad_tr_bias,
        ),
        ("samp", "head"),
    )
    return (
        block_out,
        grad_single,
        grad_pair,
        small_sums[1],
        summed[0],
        small_sums[3],
        summed[1],
        summed[2],
        small_sums[4],
        summed[3],
        summed[4],
        summed[5],
        summed[6],
        small_sums[0],
        summed[7],
        small_sums[5],
        small_sums[2],
        summed[8],
        small_sums[6],
        summed[9],
        summed[10],
        summed[11],
        summed[12],
        summed[13],
        small_sums[7],
    )


def solution(mesh):
    placed = (
        P("samp", "head", None),
        P("samp", "head", None),
        P(None, "head", "samp", None),
        P(),
        P("samp"),
        P("samp", "head", None),
        P(),
        P(),
        P(),
        P(),
        P(),
        P(),
        P(),
        P(),
        P(),
        P(),
        P(),
        P(),
        P(),
        P(),
        P(),
        P(),
        P(),
        P(),
        P(),
        P(),
        P(),
        P(),
    )
    return jax.shard_map(
        on_device,
        mesh=mesh,
        in_specs=placed,
        out_specs=(
            P("samp", "head", None),
            P("samp", "head", None),
            P(None, "head", "samp", None),
            P(),
            P("samp", "head"),
            P(),
            P("samp", "head"),
            P("samp", "head"),
            P(),
            P("samp", "head"),
            P("samp", "head"),
            P("samp", "head"),
            P("samp", "head"),
            P(),
            P("samp", "head"),
            P(),
            P(),
            P("samp", "head"),
            P(),
            P("samp", "head"),
            P("samp", "head"),
            P("samp", "head"),
            P("samp", "head"),
            P("samp", "head"),
            P(),
        ),
        check_vma=False,
    )
```

profile of v0, /device:TPU:0, one launch (start us, length us, event | category | flops | bytes accessed | tf_op | source)
XLA Modules:
  0.0 2588.1 jit_solution(2299471748566385895)
XLA Ops:
  29.3 15.8 fusion.83
  45.5 24.7 all_to_all.171
  110.5 26.6 %all-to-all-done.1 = bf16[8,192,768]{1,0,2:T(8,128)(2,1)} async-done(((bf16[8,192,768]{1,0,2:T(8,128)(2,1)}), bf16[8,192,768]{1,0,2:T(8,128)(2,1)}, u32[]{:S(2)}, u32[]{:S(2)}) %all-to-all-start.1) | async-done | bytes 2359328 | tf_op jit(solution)/shard_map/all_to_all | solution.py:134
  152.4 26.6 %all-to-all-done.2 = bf16[8,192,768]{1,0,2:T(8,128)(2,1)} async-done(((bf16[8,192,768]{1,0,2:T(8,128)(2,1)}), bf16[8,192,768]{1,0,2:T(8,128)(2,1)}, u32[]{:S(2)}, u32[]{:S(2)}) %all-to-all-start.2) | async-done | bytes 2359328 | tf_op jit(solution)/shard_map/all_to_all | solution.py:135
  234.6 126.7 %while.30 = (s32[]{:T(128)}, bf16[8,768,192]{1,2,0:T(8,128)(2,1)}, f32[8,4,768]{2,1,0:T(4,128)}, bf16[8,768,192]{1,2,0:T(8,128)(2,1)}, s32[8]{0:T(128)}, /*index...) while((s32[]{:T(128)}, bf16[8,768,192]{1,2,0:T(8,128)(2,1)}, ...), condition=%wide.region_10.11_spmd.clone, body=%wide.region_7.10_spmd.clone.sunk | while | flops 476722944 | bytes 36669136 | solution.py:160
  385.9 22.0 all-to-all-done.4
  449.4 18.2 multiply_convert_fusion.2
  518.0 33.5 %all-to-all-done.5 = bf16[8,192,768]{1,0,2:T(8,128)(2,1)} async-done(((bf16[8,192,768]{1,0,2:T(8,128)(2,1)}), bf16[8,192,768]{1,0,2:T(8,128)(2,1)}, u32[]{:S(2)}, u32[]{:S(2)}) %all-to-all-start.5) | async-done | bytes 2359328 | tf_op jit(solution)/shard_map/all_to_all | solution.py:208
  575.6 498.1 %while.31 = (s32[]{:T(128)}, f32[2,4,768,768]{2,1,0,3:T(4,128)}, bf16[8,768,192]{1,2,0:T(8,128)(2,1)}, bf16[8,768,192]{1,2,0:T(8,128)(2,1)}, bf16[8,768,192]{1,2...) while((s32[]{:T(128)}, f32[2,4,768,768]{2,1,0,3:T(4,128)}, ...), condition=%wide.region_17.18_spmd.clone, body=%wide.region_15.17_spmd.clone.sunk | while | flops 1163867904 | bytes 214759216 | solution.py:250
  605.5 15.0 fusion.246
  1091.6 32.1 %all-to-all-done.8 = bf16[8,768,192]{2,0,1:T(8,128)(2,1)} async-done(((bf16[8,768,192]{2,0,1:T(8,128)(2,1)}), bf16[8,768,192]{2,0,1:T(8,128)(2,1)}, u32[]{:S(2)}, u32[]{:S(2)}) %all-to-all-start.8) | async-done | bytes 2359328 | tf_op jit(solution)/shard_map/all_to_all | solution.py:258
  1138.3 33.4 %all-to-all-done.6 = bf16[8,768,192]{2,0,1:T(8,128)(2,1)} async-done(((bf16[8,768,192]{2,0,1:T(8,128)(2,1)}), bf16[8,768,192]{2,0,1:T(8,128)(2,1)}, u32[]{:S(2)}, u32[]{:S(2)}) %all-to-all-start.6) | async-done | bytes 2359328 | tf_op jit(solution)/shard_map/all_to_all | solution.py:256
  1347.9 15.8 reduce-scatter.65.cloned.1.call-done
  1365.8 26.4 %reduce-scatter.61.cloned.1.call-done = bf16[768,192]{0,1:T(8,128)(2,1)} async-done(((bf16[768,768]{0,1:T(8,128)(2,1)}), bf16[768,192]{0,1:T(8,128)(2,1)}) %reduce-scatter.61.cloned.1.call-update) | async-done | bytes 294928 | tf_op jit(solution)/shard_map/reduce_scatter | solution.py:290
  1394.3 26.0 %reduce-scatter.63.cloned.1.call-done = bf16[768,192]{0,1:T(8,128)(2,1)} async-done(((bf16[768,768]{0,1:T(8,128)(2,1)}), bf16[768,192]{0,1:T(8,128)(2,1)}) %reduce-scatter.63.cloned.1.call-update) | async-done | bytes 294928 | tf_op jit(solution)/shard_map/reduce_scatter | solution.py:293
  1423.7 32.4 %reduce-scatter.107.cloned.1.call-done = bf16[384,768]{1,0:T(8,128)(2,1)} async-done(((bf16[1536,768]{1,0:T(8,128)(2,1)}), bf16[384,768]{1,0:T(8,128)(2,1)}) %reduce-scatter.107.cloned.1.call-update) | async-done | bytes 589840
  1458.6 751.6 %all-reduce.3 = bf16[2,4,768,768]{2,1,0,3:T(4,128)(2,1)} all-reduce(f32[2,4,768,768]{2,1,0,3:T(4,128)} %get-tuple-element.158), channel_id=2, replica_groups=mesh['samp'=8,'head'=4] {'samp'}, use_global_device_ids=true, to_apply=%region_20.21.clone | all-reduce | flops 4718592 | bytes 28311552
  2241.0 32.4 %fusion.142 = (f32[2,192,96]{2,1,0:T(8,128)S(1)}, f32[2,192,96]{2,1,0:T(8,128)S(1)}, f32[2,192,96,128]{3,2,1,0:T(8,128)}) fusion(f32[2,192,96]{2,1,0:T(8,128)S(1)} %copy-done.23, f32[2,192,96]{2,1,0:T(8,128)S(1)} %copy-done.21, bf16[2,192,96,128]{3,2,1,0:T(8,128)(2,1)} %param.34, bf16[2,16,192,96]{3,1,2,0:T(8,128)(2,1)S(1)} %bitcast.389, ...), kind=kOutput, calls=%fused_computation.217 | convolution fusion | flops 179232768 | bytes 30085120 | tf_op jit(solution)/shard_map/chij,zh->cijz/dot_general | solution.py:281
  2276.1 25.5 fusion.27
  2301.6 17.6 fusion.113
  2329.8 38.5 %all-reduce.1 = (f32[384]{0:T(512)}, f32[768]{0:T(1024)}, f32[768]{0:T(1024)}, f32[128,16]{0,1:T(8,128)}, f32[768]{0:T(1024)}, /*index=5*/f32[384]{0:T(512)}, f32[768]{0:T(1024)}, f32[768]{0:T(1024)}) all-reduce(f32[384]{0:T(512)} %fusion.62, f32[768]{0:T(1024)} %get-tuple-element.373, ...), channel_id=1, replica_groups=mesh['samp'=8,'head'=4] {'samp','head'}, use_global_device_ids=true, to_apply=%region_24.25 | all-reduce | flops 6656 | bytes 53248 | tf_op jit(solution)/shard_map/psum | solution.py:343
  2378.5 67.2 %reduce-scatter.79.cloned.1.call-done = f32[96,384]{1,0:T(8,128)} async-done(((f32[768,384]{1,0:T(8,128)}), f32[96,384]{1,0:T(8,128)}) %reduce-scatter.79.cloned.1.call-update) | async-done | bytes 147472 | tf_op jit(solution)/shard_map/reduce_scatter | solution.py:339
  2445.8 67.3 %reduce-scatter.77.cloned.1.call-done = f32[96,384]{1,0:T(8,128)} async-done(((f32[768,384]{1,0:T(8,128)}), f32[96,384]{1,0:T(8,128)}) %reduce-scatter.77.cloned.1.call-update) | async-done | bytes 147472 | tf_op jit(solution)/shard_map/reduce_scatter | solution.py:338
  2513.1 68.3 %reduce-scatter.109.cloned.1.call-done = f32[192,192]{1,0:T(8,128)} async-done(((f32[1536,192]{1,0:T(8,128)}), f32[192,192]{1,0:T(8,128)}) %reduce-scatter.109.cloned.1.call-update) | async-done | bytes 147472
  (651 shorter events, 1121.8 us)
Async XLA Ops:
  7.2 225.8 %all-gather.2.cloned.1.call-start = ((), (), s32[]{:S(2)}) async-start(), calls=%async_computation.38 | async-start | bytes 10616832 | tf_op jit(solution)/shard_map/all_gather | solution.py:119
  511.4 820.8 %reduce-scatter.71.cloned.1.call-start = ((), (), s32[]{:S(2)}) async-start(), calls=%async_computation.46 | async-start | bytes 737280 | tf_op jit(solution)/shard_map/reduce_scatter | solution.py:305
  513.8 820.3 %reduce-scatter.73.cloned.1.call-start = ((), (), s32[]{:S(2)}) async-start(), calls=%async_computation.47 | async-start | bytes 737280 | tf_op jit(solution)/shard_map/reduce_scatter | solution.py:308
  1083.5 252.5 %reduce-scatter.75.cloned.1.call-start = ((), (), s32[]{:S(2)}) async-start(), calls=%async_computation.48 | async-start | bytes 737280 | tf_op jit(solution)/shard_map/reduce_scatter | solution.py:311
  1128.3 209.6 %reduce-scatter.69.cloned.1.call-start = ((), (), s32[]{:S(2)}) async-start(), calls=%async_computation.45 | async-start | bytes 1474560 | tf_op jit(solution)/shard_map/reduce_scatter | solution.py:302
  1176.3 163.7 %reduce-scatter.67.cloned.1.call-start = ((), (), s32[]{:S(2)}) async-start(), calls=%async_computation.44 | async-start | bytes 1474560 | tf_op jit(solution)/shard_map/reduce_scatter | solution.py:299
  1181.2 161.0 %reduce-scatter.83.cloned.1.call-start = ((), (), s32[]{:S(2)}) async-start(), calls=%async_computation.52 | async-start | bytes 737280 | tf_op jit(solution)/shard_map/reduce_scatter | solution.py:323
  1302.0 154.2 %reduce-scatter.107.cloned.1.call-start = ((), (), s32[]{:S(2)}) async-start(), calls=%async_computation.64 | async-start | bytes 2949120
  1312.0 906.2 %reduce-scatter.105.cloned.1.call-start = ((), (), s32[]{:S(2)}) async-start(), calls=%async_computation.63 | async-start | bytes 2949120
  1321.4 952.1 %reduce-scatter.81.cloned.1.call-start = ((), (), s32[]{:S(2)}) async-start(), calls=%async_computation.51 | async-start | bytes 2949120 | tf_op jit(solution)/shard_map/reduce_scatter | solution.py:320
  1332.2 1036.2 %reduce-scatter.99.cloned.1.call-start = ((), (), s32[]{:S(2)}) async-start(), calls=%async_computation.60 | async-start | bytes 442368
  1334.1 1034.3 %reduce-scatter.101.cloned.1.call-start = ((), (), s32[]{:S(2)}) async-start(), calls=%async_computation.61 | async-start | bytes 442368
  1336.0 1032.4 %reduce-scatter.103.cloned.1.call-start = ((), (), s32[]{:S(2)}) async-start(), calls=%async_computation.62 | async-start | bytes 442368
  1337.9 1030.5 %reduce-scatter.97.cloned.1.call-start = ((), (), s32[]{:S(2)}) async-start(), calls=%async_computation.59 | async-start | bytes 884736
  1340.0 1028.4 %reduce-scatter.95.cloned.1.call-start = ((), (), s32[]{:S(2)}) async-start(), calls=%async_computation.58 | async-start | bytes 884736
  1342.1 1026.3 %reduce-scatter.111.cloned.1.call-start = ((), (), s32[]{:S(2)}) async-start(), calls=%async_computation.66 | async-start | bytes 442368
  1344.1 1024.4 %reduce-scatter.85.cloned.1.call-start = ((), (), s32[]{:S(2)}) async-start(), calls=%async_computation.53 | async-start | bytes 442368
  1346.0 1022.5 %reduce-scatter.87.cloned.1.call-start = ((), (), s32[]{:S(2)}) async-start(), calls=%async_computation.54 | async-start | bytes 442368
  1347.9 1020.6 %reduce-scatter.93.cloned.1.call-start = ((), (), s32[]{:S(2)}) async-start(), calls=%async_computation.57 | async-start | bytes 884736
  1365.8 1002.7 %reduce-scatter.89.cloned.1.call-start = ((), (), s32[]{:S(2)}) async-start(), calls=%async_computation.55 | async-start | bytes 884736
  1394.3 984.3 %reduce-scatter.91.cloned.1.call-start = ((), (), s32[]{:S(2)}) async-start(), calls=%async_computation.56 | async-start | bytes 884736
  1422.4 1023.4 %reduce-scatter.79.cloned.1.call-start = ((), (), s32[]{:S(2)}) async-start(), calls=%async_computation.50 | async-start | bytes 1327104 | tf_op jit(solution)/shard_map/reduce_scatter | solution.py:339
  2217.9 295.2 %reduce-scatter.77.cloned.1.call-start = ((), (), s32[]{:S(2)}) async-start(), calls=%async_computation.49 | async-start | bytes 1327104 | tf_op jit(solution)/shard_map/reduce_scatter | solution.py:338
  2220.6 360.8 %reduce-scatter.109.cloned.1.call-start = ((), (), s32[]{:S(2)}) async-start(), calls=%async_computation.65 | async-start | bytes 1769472
  (116 other events, 3235.1 us)
Sparse Core Ops, SparseCore 0:
  78.5 138.8 all-gather.1
  514.7 27.6 reduce-scatter.70
  1088.1 27.5 reduce-scatter.74
  1133.4 34.3 reduce-scatter.68
  1181.3 34.3 reduce-scatter.66
  1338.0 25.7 reduce-scatter.64
  1366.5 25.7 reduce-scatter.60
  1423.1 33.0 reduce-scatter.106
  1458.5 33.0 reduce-scatter.104
  1494.1 33.0 reduce-scatter.80
  1530.9 80.2 reduce-scatter.98
  1614.9 75.3 reduce-scatter.100
  1694.1 76.2 reduce-scatter.102
  1774.3 74.2 reduce-scatter.96
  1852.6 90.3 reduce-scatter.94
  1946.9 77.5 reduce-scatter.110
  2028.4 71.7 reduce-scatter.84
  2103.9 77.4 reduce-scatter.86
  2185.2 62.3 reduce-scatter.92
  2251.8 61.4 reduce-scatter.88
  2317.0 61.4 reduce-scatter.90
  2382.7 62.9 reduce-scatter.78
  2450.1 62.9 reduce-scatter.76
  2517.5 63.8 reduce-scatter.108
  (5 shorter events, 114.6 us)
where the time goes:
time: 2600 us; the launch traced here: 2590 us
  blocking collectives  815 us (31%)
  local copies, waits for them, and re-layouts  526 us (20%)
  waiting for transfers between devices  514 us (20%)
  matrix products  428 us (16%)
  other arithmetic  214 us (8%)
  starting transfers between devices  42.6 us (2%)
  loops' own time  32.8 us (1%)
    unnamed x1, blocking collectives  752 us
    broadcast_in_dim x8, other arithmetic, attend_back(): lax.dynamic_update_index_in_dim(bias_grad, previous + d_scores.astype(jnp...  120 us
    unnamed x43, waiting for transfers between devices  111 us
    dynamic_update_slice x8, local copies, waits for them, and re-layouts, attend_back(): lax.dynamic_update_index_in_dim(bias_grad, previous + d_scores.astype(jnp...  108 us
    dot_general x16, matrix products, score_block(): jnp.einsum('ihd,jhd->hij', query_split, key_split, preferred_element_type...  91.7 us
    dot_general x14, matrix products, project(): return jnp.dot(inputs, weight, preferred_element_type=jnp.float32)  80.2 us
    dynamic_slice x80, local copies, waits for them, and re-layouts, on_device(): lax.map(attend, (query_heads, key_heads, value_heads, sample_complex, len...  77.4 us
    dynamic_slice x8, local copies, waits for them, and re-layouts, attend_back(): lax.dynamic_index_in_dim(bias_grad, complex_id, 0, keepdims=False)  71.5 us
  transfers between devices with their start and end apart: 38, of which 17 were waited for; matrix products, arithmetic and copies ran while one was open for 32% of the time, Pallas kernels for 0%

commit v1 on v0

v1 whole, which is shorter than its diff:
```python
import functools
import math

import jax
import jax.numpy as jnp
from jax import lax
from jax.experimental import pallas as pl
from jax.experimental.pallas import tpu as pltpu
from jax.sharding import PartitionSpec as P

f32, bf16 = jnp.float32, jnp.bfloat16
epsilon = 1e-05
fill_value = -1e30
LOG2E = math.log2(math.e)
VMEM_BYTES = 60 << 20
NN, NT, TN = ((1,), (0,)), ((1,), (1,)), ((0,), (0,))


def dot(a, b, dims):
    return lax.dot_general(a, b, (dims, ((), ())), preferred_element_type=f32)


def norm_rows(inputs):
    mean_val = jnp.mean(inputs, axis=-1, keepdims=True)
    centered = inputs - mean_val
    variance = jnp.mean(centered * centered, axis=-1, keepdims=True)
    inverse = lax.rsqrt(variance + epsilon)
    return (centered * inverse, inverse)


def norm_back(normed, inverse, upstream):
    mean_grad = jnp.mean(upstream, axis=-1, keepdims=True)
    mean_dot = jnp.mean(upstream * normed, axis=-1, keepdims=True)
    return inverse * (upstream - mean_grad - normed * mean_dot)


def tile_of(tokens):
    return max(t for t in (8, 16, 32, 64, 128, 256) if tokens % t == 0)


def attend_kernel(meta, x0, x1, x2, x3, w_ref, bq_ref, bias_ref, o_ref, p_ref, q_ref, k_ref, v_ref, l_ref,
                  xs, ks, ss, *, nh, hd, rows, jc, nchunk, per_block, qscale):
    b = pl.program_id(0)
    g = meta[0]
    cplx = meta[1 + b]
    for r, x in enumerate((x0, x1, x2, x3)):
        xs[r * rows:(r + 1) * rows, :] = x[0]
    wch = nh * hd
    q = dot(w_ref[0:wch, :], xs[0:2 * rows, :], NT) + bq_ref[...]
    q_ref[0] = (q * qscale).astype(bf16)
    kv = dot(w_ref[wch:3 * wch, :], xs[...], NT).astype(bf16)
    k_ref[0] = kv[0:wch]
    v_ref[0] = kv[wch:]
    ones = jnp.ones((16, kv.shape[1]), bf16)
    outs = []
    sums = []
    for h in range(nh):
        ks[h % 2, :, :] = jnp.transpose(k_ref[0, h * hd:(h + 1) * hd, :])
        qT = q_ref[0, h * hd:(h + 1) * hd, :]
        m = None
        for t in range(nchunk):
            r, u = t // per_block, t % per_block
            s_idx = (r ^ g) * per_block + u
            s = dot(ks[h % 2, t * jc:(t + 1) * jc, :], qT, NN) + bias_ref[s_idx, cplx, h].astype(f32)
            ss[h % 2, t * jc:(t + 1) * jc, :] = s
            mt = jnp.max(s.reshape(jc // 8, 8, s.shape[1]), axis=0)
            m = mt if m is None else jnp.maximum(m, mt)
        m = jnp.max(m, axis=0, keepdims=True)
        for t in range(nchunk):
            p_ref[0, h, t * jc:(t + 1) * jc, :] = jnp.exp2(ss[h % 2, t * jc:(t + 1) * jc, :] - m).astype(bf16)
        va = jnp.concatenate([v_ref[0, h * hd:(h + 1) * hd, :], ones], axis=0)
        oT = dot(va, p_ref[0, h], NN)
        l = oT[hd:hd + 1, :]
        outs.append(oT[:hd] / l)
        sums.append(l)
    l_ref[0] = jnp.concatenate(sums, axis=0)
    o = jnp.transpose(jnp.concatenate(outs, axis=0)).astype(bf16)
    o_ref[0, 0] = o[:rows]
    o_ref[1, 0] = o[rows:]

def attend(meta, xb, wT, bq, bias, *, nh, hd):
    B, rows, C = xb[0].shape
    nchunk, ncx, _, jc, qi = bias.shape
    L = nchunk * jc
    wch = nh * hd
    kern = functools.partial(attend_kernel, nh=nh, hd=hd, rows=rows, jc=jc, nchunk=nchunk, per_block=nchunk // 4, qscale=LOG2E / math.sqrt(hd))
    xspec = pl.BlockSpec((1, rows, C), lambda b, m: (b, 0, 0))
    const = lambda shape: pl.BlockSpec(shape, lambda b, m: (0,) * len(shape), pipeline_mode=pl.Buffered(1))
    per = lambda shape: pl.BlockSpec((1,) + shape, lambda b, m: (b,) + (0,) * len(shape))
    return pl.pallas_call(
        kern,
        grid_spec=pltpu.PrefetchScalarGridSpec(
            num_scalar_prefetch=1, grid=(B,),
            in_specs=[xspec] * 4 + [const(wT.shape), const(bq.shape), const(bias.shape)],
            out_specs=[pl.BlockSpec((2, 1, rows, wch), lambda b, m: (0, b, 0, 0)), per((nh, L, qi)), per((wch, qi)), per((wch, L)), per((wch, L)), per((nh, qi))],
            scratch_shapes=[pltpu.VMEM((L, C), bf16), pltpu.VMEM((2, L, hd), bf16), pltpu.VMEM((2, L, qi), f32)],
        ),
        out_shape=[jax.ShapeDtypeStruct((2, B, rows, wch), bf16), jax.ShapeDtypeStruct((B, nh, L, qi), bf16),
                   jax.ShapeDtypeStruct((B, wch, qi), bf16), jax.ShapeDtypeStruct((B, wch, L), bf16), jax.ShapeDtypeStruct((B, wch, L), bf16),
                   jax.ShapeDtypeStruct((B, nh, qi), f32)],
        compiler_params=pltpu.CompilerParams(vmem_limit_bytes=VMEM_BYTES),
        cost_estimate=pl.CostEstimate(flops=int(30e9), bytes_accessed=int(60e6), transcendentals=int(9e6)),
        name="attend",
    )(meta, *xb, wT, bq, bias)

def attend_back_kernel(meta, x0, x1, x2, x3, w_ref, p_ref, q_ref, k_ref, v_ref, l_ref, o_ref, do0, do1, *rest,
                       nh, hd, rows, jc, nchunk, per_block, scale, chained):
    before = rest[0] if chained else None
    dx_ref, db_ref, gw_ref, gb_ref, xs, vs, ds, acc, dst = rest[1:] if chained else rest
    b = pl.program_id(0)
    g = meta[0]
    cplx = meta[1 + b]
    wch = nh * hd
    L = nchunk * jc

    @pl.when(b == 0)
    def _():
        acc[...] = jnp.zeros_like(acc)
        gw_ref[...] = jnp.zeros_like(gw_ref)
        gb_ref[...] = jnp.zeros_like(gb_ref)

    for r, x in enumerate((x0, x1, x2, x3)):
        xs[r * rows:(r + 1) * rows, :] = x[0]
    dO = jnp.transpose(jnp.concatenate([do0[0], do1[0]], axis=0).astype(f32))
    O = jnp.transpose(jnp.concatenate([o_ref[0, 0], o_ref[1, 0]], axis=0).astype(f32))
    prod = dO * O
    qi = dO.shape[1]
    row = lax.broadcasted_iota(jnp.int32, (16, qi), 0)
    ones = jnp.ones((16, L), bf16)
    for h in range(nh):
        hs = slice(h * hd, (h + 1) * hd)
        linv = 1.0 / l_ref[0, h:h + 1, :]
        dOh = (dO[hs] * linv).astype(bf16)
        delta = jnp.sum(prod[hs], axis=0, keepdims=True) * linv
        hi = delta.astype(bf16).astype(f32)
        extra = jnp.where(row == 0, -hi, jnp.where(row == 1, hi - delta, 0.0)).astype(bf16)
        dOa = jnp.concatenate([dOh, extra], axis=0)
        vs[h % 2] = jnp.transpose(jnp.concatenate([v_ref[0, hs, :], ones], axis=0))
        for t in range(nchunk):
            r, u = t // per_block, t % per_block
            s_idx = (r ^ g) * per_block + u
            ts = slice(t * jc, (t + 1) * jc)
            d = dot(vs[h % 2, ts, :], dOa, NN) * p_ref[0, h, ts, :].astype(f32)
            acc[s_idx, cplx, h] += d
            ds[h % 2, ts, :] = d.astype(bf16)
        dst[h * hd:(h + 1) * hd, 0:qi] = (dot(k_ref[0, hs, :], ds[h % 2], NN) * scale).astype(bf16)
        dst[wch + h * hd:wch + (h + 1) * hd, :] = (dot(q_ref[0, hs, :], ds[h % 2], NT) * (1.0 / LOG2E)).astype(bf16)
        dst[2 * wch + h * hd:2 * wch + (h + 1) * hd, :] = dot(dOh, p_ref[0, h], NT).astype(bf16)
    dq = dst[0:wch, 0:qi]
    gb_ref[...] += jnp.sum(dq.astype(f32), axis=1, keepdims=True)
    gw_ref[0:wch, :] += dot(dq, xs[0:qi, :], NN)
    gw_ref[wch:, :] += dot(dst[wch:, :], xs[...], NN)
    dkv = jnp.transpose(dst[wch:, :])
    dqr = jnp.transpose(dq)
    for r in range(4):
        rs = slice(r * rows, (r + 1) * rows)
        dx = dot(dkv[rs], w_ref[wch:, :], NN)
        if r < 2:
            dx += dot(dqr[rs], w_ref[0:wch, :], NN)
        if chained:
            dx += before[r, 0].astype(f32)
        dx_ref[r, 0] = dx.astype(bf16)

    @pl.when(b == pl.num_programs(0) - 1)
    def _():
        db_ref[...] = acc[...].astype(bf16)

def attend_back(meta, xb, wT, p, q, k, v, l, o, do0, do1, before, nchunk, ncx, *, nh, hd):
    B, rows, C = xb[0].shape
    L = k.shape[2]; qi = q.shape[2]; jc = L // nchunk
    wch = nh * hd
    kern = functools.partial(attend_back_kernel, nh=nh, hd=hd, rows=rows, jc=jc, nchunk=nchunk, per_block=nchunk // 4, scale=1.0 / math.sqrt(hd), chained=before is not None)
    xspec = pl.BlockSpec((1, rows, C), lambda b, m: (b, 0, 0))
    const = lambda shape: pl.BlockSpec(shape, lambda b, m: (0,) * len(shape), pipeline_mode=pl.Buffered(1))
    per = lambda shape: pl.BlockSpec((1,) + shape, lambda b, m: (b,) + (0,) * len(shape))
    db = (nchunk, ncx, nh, jc, qi)
    blockspec = pl.BlockSpec((4, 1, rows, C), lambda b, m: (0, b, 0, 0))
    extra = () if before is None else (before,)
    return pl.pallas_call(
        kern,
        grid_spec=pltpu.PrefetchScalarGridSpec(
            num_scalar_prefetch=1, grid=(B,),
            in_specs=[xspec] * 4 + [const(wT.shape), per((nh, L, qi)), per((wch, qi)), per((wch, L)), per((wch, L)), per((nh, qi)),
                      pl.BlockSpec((2, 1, rows, wch), lambda b, m: (0, b, 0, 0)), per((rows, wch)), per((rows, wch))]
            + [blockspec] * (before is not None),
            out_specs=[blockspec, const(db), const((3 * wch, C)), const((wch, 1))],
            scratch_shapes=[pltpu.VMEM((L, C), bf16), pltpu.VMEM((2, L, hd + 16), bf16), pltpu.VMEM((2, L, qi), bf16), pltpu.VMEM(db, f32), pltpu.VMEM((3 * wch, L), bf16)],
        ),
        out_shape=[jax.ShapeDtypeStruct((4, B, rows, C), bf16), jax.ShapeDtypeStruct(db, bf16), jax.ShapeDtypeStruct((3 * wch, C), f32), jax.ShapeDtypeStruct((wch, 1), f32)],
        compiler_params=pltpu.CompilerParams(vmem_limit_bytes=VMEM_BYTES),
        cost_estimate=pl.CostEstimate(flops=int(60e9), bytes_accessed=int(60e6), transcendentals=0),
        name="attend_back",
    )(meta, *xb, wT, p, q, k, v, l, o, do0, do1, *extra)


def fold8(v):
    return jnp.sum(v.reshape(v.shape[0] // 8, 8, v.shape[1]), axis=0)


def fixed(shape):
    return pl.BlockSpec(shape, lambda *_: (0,) * len(shape), pipeline_mode=pl.Buffered(1))


def tiled(rows, width):
    return pl.BlockSpec((rows, width), lambda t, *_: (t, 0))


def adapt_kernel(single_ref, cond_ref, gain, w_scale, b_scale, w_shift, x_ref):
    normed, _ = norm_rows(single_ref[...].astype(f32))
    cond_hat, _ = norm_rows(cond_ref[...].astype(f32))
    cond_low = (cond_hat * gain[...].astype(f32)).astype(bf16)
    gate = jax.nn.sigmoid(dot(cond_low, w_scale[...], NN) + b_scale[...].astype(f32))
    x_ref[...] = (gate * normed + dot(cond_low, w_shift[...], NN)).astype(bf16)


def adapt(single, cond, gain, w_scale, b_scale, w_shift):
    tokens, width = single.shape
    tile = tile_of(tokens)
    return pl.pallas_call(
        adapt_kernel,
        grid=(tokens // tile,),
        in_specs=[tiled(tile, width), tiled(tile, cond.shape[1])]
        + [fixed(v.shape) for v in (gain, w_scale, b_scale, w_shift)],
        out_specs=tiled(tile, width),
        out_shape=jax.ShapeDtypeStruct((tokens, width), bf16),
        compiler_params=pltpu.CompilerParams(vmem_limit_bytes=VMEM_BYTES),
        cost_estimate=pl.CostEstimate(
            flops=4 * tokens * width * cond.shape[1], bytes_accessed=8 * tokens * width, transcendentals=tokens * width
        ),
        name="adapt",
    )(single, cond, gain, w_scale, b_scale, w_shift)


def middle_kernel(
    meta, x_ref, single_ref, cond_ref, cot_ref, a0, a1, a2, a3,
    w_gate, w_out, w_ac, b_ac, gain, w_scale, b_scale, w_shift, w_hg, w_hu, w_dn, w_tc, b_tc,
    out_ref, dmid_ref, dxg_ref, da0, da1, da2, da3,
    g_gate, g_out, g_ac, g_scale, g_shift, g_hg, g_hu, g_dn, g_tc, s_ac, s_scale, s_tc, s_gain,
):
    core = meta[0] % 2

    @pl.when(pl.program_id(0) == 0)
    def _():
        for ref in (g_gate, g_out, g_ac, g_scale, g_shift, g_hg, g_hu, g_dn, g_tc, s_ac, s_scale, s_tc, s_gain):
            ref[...] = jnp.zeros_like(ref)

    x_one = x_ref[...]
    cond = cond_ref[...]
    gate = jax.nn.sigmoid(dot(x_one, w_gate[...], NN))
    first = core == 0
    att = jnp.concatenate(
        [
            jnp.where(first, a0[...], a1[...]),
            jnp.where(first, a1[...], a0[...]),
            jnp.where(first, a2[...], a3[...]),
            jnp.where(first, a3[...], a2[...]),
        ],
        axis=1,
    ).astype(f32)
    gated = (att * gate).astype(bf16)
    branch = dot(gated, w_out[...], NN)
    acond = jax.nn.sigmoid(dot(cond, w_ac[...], NN) + b_ac[...].astype(f32))
    mid = single_ref[...].astype(f32) + acond * branch
    cond_hat, _ = norm_rows(cond.astype(f32))
    cond_low = (cond_hat * gain[...].astype(f32)).astype(bf16)
    scale = jax.nn.sigmoid(dot(cond_low, w_scale[...], NN) + b_scale[...].astype(f32))
    normed, inverse = norm_rows(mid)
    x_two = (scale * normed + dot(cond_low, w_shift[...], NN)).astype(bf16)
    hgate = dot(x_two, w_hg[...], NN)
    hup = dot(x_two, w_hu[...], NN)
    sig = jax.nn.sigmoid(hgate)
    silu = hgate * sig
    hidden = (silu * hup).astype(bf16)
    tr_branch = dot(hidden, w_dn[...], NN)
    tcond = jax.nn.sigmoid(dot(cond, w_tc[...], NN) + b_tc[...].astype(f32))
    out_ref[...] = (mid + tcond * tr_branch).astype(bf16)
    dy = cot_ref[...].astype(f32)
    d_tr = (tcond * dy).astype(bf16)
    d_trc = dy * tr_branch * tcond * (1.0 - tcond)
    s_tc[...] += fold8(d_trc)
    g_tc[...] += dot(cond, d_trc.astype(bf16), TN)
    g_dn[...] += dot(hidden, d_tr, TN)
    d_hidden = dot(d_tr, w_dn[...], NT)
    d_hg = (d_hidden * hup * sig * (1.0 + hgate * (1.0 - sig))).astype(bf16)
    d_hu = (d_hidden * silu).astype(bf16)
    g_hg[...] += dot(x_two, d_hg, TN)
    g_hu[...] += dot(x_two, d_hu, TN)
    g_two = dot(d_hg, w_hg[...], NT) + dot(d_hu, w_hu[...], NT)
    d_scale = g_two * normed * scale * (1.0 - scale)
    s_scale[...] += fold8(d_scale)
    d_scale = d_scale.astype(bf16)
    d_shift = g_two.astype(bf16)
    g_scale[...] += dot(cond_low, d_scale, TN)
    g_shift[...] += dot(cond_low, d_shift, TN)
    d_cond = dot(d_scale, w_scale[...], NT) + dot(d_shift, w_shift[...], NT)
    s_gain[...] += fold8(d_cond * cond_hat)
    d_mid = dy + norm_back(normed, inverse, g_two * scale)
    dmid_ref[...] = d_mid
    d_attn = (acond * d_mid).astype(bf16)
    d_ac = d_mid * branch * acond * (1.0 - acond)
    s_ac[...] += fold8(d_ac)
    g_ac[...] += dot(cond, d_ac.astype(bf16), TN)
    g_out[...] += dot(gated, d_attn, TN)
    d_gated = dot(d_attn, w_out[...], NT)
    d_att = (d_gated * gate).astype(bf16)
    d_gate = (d_gated * att * gate * (1.0 - gate)).astype(bf16)
    g_gate[...] += dot(x_one, d_gate, TN)
    dxg_ref[...] = dot(d_gate, w_gate[...], NT).astype(bf16)
    q = d_att.shape[1] // 4
    parts = [d_att[:, i * q : (i + 1) * q] for i in range(4)]
    da0[...] = jnp.where(first, parts[0], parts[1])
    da1[...] = jnp.where(first, parts[1], parts[0])
    da2[...] = jnp.where(first, parts[2], parts[3])
    da3[...] = jnp.where(first, parts[3], parts[2])


def middle(meta, x_one, single, cond, cot, atts, weights):
    tokens, width = single.shape
    tile = tile_of(tokens)
    cs = cond.shape[1]
    quarter = atts[0].shape[1]
    w_gate, w_out, w_ac, b_ac, gain, w_scale, b_scale, w_shift, w_hg, w_hu, w_dn, w_tc, b_tc = weights
    total = lambda w: jax.ShapeDtypeStruct(w.shape, f32)
    fold = lambda n: jax.ShapeDtypeStruct((8, n), f32)
    grads = [total(w) for w in (w_gate, w_out, w_ac, w_scale, w_shift, w_hg, w_hu, w_dn, w_tc)] + [
        fold(width), fold(width), fold(width), fold(cs)]
    row_out = [((width,), bf16), ((width,), f32), ((width,), bf16)] + [((quarter,), bf16)] * 4
    macs = sum(w.size for w in weights if w.shape[0] > 1)
    return pl.pallas_call(
        middle_kernel,
        grid_spec=pltpu.PrefetchScalarGridSpec(
            num_scalar_prefetch=1,
            grid=(tokens // tile,),
            in_specs=[tiled(tile, width), tiled(tile, width), tiled(tile, cs), tiled(tile, width)]
            + [tiled(tile, quarter)] * 4
            + [fixed(w.shape) for w in weights],
            out_specs=[tiled(tile, w[0]) for w, _ in row_out] + [fixed(g.shape) for g in grads],
        ),
        out_shape=[jax.ShapeDtypeStruct((tokens, w[0]), d) for w, d in row_out] + grads,
        compiler_params=pltpu.CompilerParams(vmem_limit_bytes=VMEM_BYTES),
        cost_estimate=pl.CostEstimate(flops=6 * tokens * macs, bytes_accessed=60 << 20, transcendentals=8 * tokens * width),
        name="middle",
    )(meta, x_one, single, cond, cot, *atts, *weights)


def last_kernel(d0, d1, d2, d3, single_ref, cond_ref, dmid_ref, gain, w_scale, b_scale, w_shift,
                out_ref, g_scale, g_shift, s_scale, s_gain):
    @pl.when(pl.program_id(0) == 0)
    def _():
        for ref in (g_scale, g_shift, s_scale, s_gain):
            ref[...] = jnp.zeros_like(ref)

    g_one = d0[...].astype(f32) + d1[...].astype(f32) + d2[...].astype(f32) + d3[...].astype(f32)
    normed, inverse = norm_rows(single_ref[...].astype(f32))
    cond_hat, _ = norm_rows(cond_ref[...].astype(f32))
    cond_low = (cond_hat * gain[...].astype(f32)).astype(bf16)
    scale = jax.nn.sigmoid(dot(cond_low, w_scale[...], NN) + b_scale[...].astype(f32))
    d_scale = g_one * normed * scale * (1.0 - scale)
    s_scale[...] += fold8(d_scale)
    d_scale = d_scale.astype(bf16)
    d_shift = g_one.astype(bf16)
    g_scale[...] += dot(cond_low, d_scale, TN)
    g_shift[...] += dot(cond_low, d_shift, TN)
    d_cond = dot(d_scale, w_scale[...], NT) + dot(d_shift, w_shift[...], NT)
    s_gain[...] += fold8(d_cond * cond_hat)
    out_ref[...] = dmid_ref[...] + norm_back(normed, inverse, g_one * scale)


def last(ds, single, cond, dmid, gain, w_scale, b_scale, w_shift):
    tokens, width = single.shape
    tile = tile_of(tokens)
    cs = cond.shape[1]
    grads = [jax.ShapeDtypeStruct(s, f32) for s in (w_scale.shape, w_shift.shape, (8, width), (8, cs))]
    return pl.pallas_call(
        last_kernel,
        grid=(tokens // tile,),
        in_specs=[tiled(tile, width)] * 5
        + [tiled(tile, cs), tiled(tile, width)]
        + [fixed(w.shape) for w in (gain, w_scale, b_scale, w_shift)],
        out_specs=[tiled(tile, width)] + [fixed(g.shape) for g in grads],
        out_shape=[jax.ShapeDtypeStruct((tokens, width), f32)] + grads,
        compiler_params=pltpu.CompilerParams(vmem_limit_bytes=VMEM_BYTES),
        cost_estimate=pl.CostEstimate(flops=12 * tokens * width * cs, bytes_accessed=30 << 20, transcendentals=tokens * width),
        name="last",
    )(*ds, single, cond, dmid, gain, w_scale, b_scale, w_shift)


def swap(value, bit):
    size = lax.axis_size("head")
    return lax.ppermute(value, "head", [(i, i ^ bit) for i in range(size)])


def on_device(
    single,
    cond,
    pair,
    complex_length,
    sample_complex,
    cotangent,
    gain_one,
    w_scale_one,
    b_scale_one,
    w_shift_one,
    w_query,
    b_query,
    w_key,
    w_value,
    w_gate,
    w_out,
    w_pair,
    w_attn_cond,
    b_attn_cond,
    gain_two,
    w_scale_two,
    b_scale_two,
    w_shift_two,
    w_hidden_gate,
    w_hidden_up,
    w_hidden_down,
    w_tr_cond,
    b_tr_cond,
):
    groups = lax.axis_size("head")
    devices = lax.axis_size("samp")
    me = lax.axis_index("head")
    core = me % 2
    part = me // 2
    samples, rows, width = single.shape
    cs = cond.shape[2]
    tokens = samples * rows
    length = rows * groups
    heads = w_pair.shape[1]
    few = heads // groups
    dim = width // heads
    wide = few * dim
    complexes, _, columns, _ = pair.shape
    chunks = 2 * groups
    chunk = length // chunks

    pair_normed, pair_inverse = norm_rows(pair.astype(f32))
    pair_low = pair_normed.astype(bf16)
    bias = jnp.einsum("cijz,zh->chji", pair_low, w_pair, preferred_element_type=f32)
    column = lax.axis_index("samp") * columns + jnp.arange(columns)
    valid = column[None, :] < complex_length[:, None]
    bias = jnp.where(valid[:, None, :, None], bias * LOG2E, fill_value).astype(bf16)
    bias = bias.reshape(complexes, groups // 2, 2, few, columns, rows)
    mine = lax.dynamic_index_in_dim(bias, core, 2, keepdims=False)
    other = lax.dynamic_index_in_dim(bias, 1 - core, 2, keepdims=False)
    bias_rows = jnp.concatenate([mine, swap(other, 1)], axis=-1)

    def regroup(gathered):
        if columns == chunk:
            return gathered
        moved = gathered.transpose(1, 2, 0, 3, 4).reshape(complexes, few, chunks, chunk, 2 * rows)
        return moved.transpose(2, 0, 1, 3, 4)

    def ungroup(summed):
        if columns == chunk:
            return summed
        moved = summed.transpose(1, 2, 0, 3, 4).reshape(complexes, few, devices, columns, 2 * rows)
        return moved.transpose(2, 0, 1, 3, 4)

    biases = [regroup(lax.all_gather(bias_rows[:, k], "samp", axis=0)) for k in range(groups // 2)]

    single_t = single.reshape(tokens, width)
    cond_t = cond.reshape(tokens, cs)
    cot_t = cotangent.reshape(tokens, width)
    line = lambda v: v.reshape(1, -1)
    x_one = adapt(single_t, cond_t, line(gain_one), w_scale_one, line(b_scale_one), w_shift_one)
    x_far = swap(x_one, 2)
    x_near = swap(x_one, 1)
    x_cross = swap(x_far, 1)
    blocks = [v.reshape(samples, rows, width) for v in (x_one, x_near, x_far, x_cross)]

    meta = jnp.concatenate([me[None].astype(jnp.int32), sample_complex])

    def own_columns(w, k):
        return lax.dynamic_slice_in_dim(w, (2 * k + core) * wide, wide, w.ndim - 1)

    w_heads = [
        jnp.concatenate([own_columns(w, k).T for w in (w_query, w_key, w_value)], axis=0) for k in range(groups // 2)
    ]
    b_heads = [own_columns(b_query.astype(f32), k)[:, None] for k in range(groups // 2)]
    kept = [attend(meta, blocks, w_heads[k], b_heads[k], biases[k], nh=few, hd=dim) for k in range(groups // 2)]
    atts = []
    for k in range(groups // 2):
        out = kept[k][0]
        atts += [out[0].reshape(tokens, wide), swap(out[1], 1).reshape(tokens, wide)]

    (
        block_out, d_mid, d_xg, da0, da1, da2, da3,
        g_gate, g_out, g_ac, g_scale2, g_shift2, g_hg, g_hu, g_dn, g_tc, s_ac, s_scale2, s_tc, s_gain2,
    ) = middle(
        meta, x_one, single_t, cond_t, cot_t, atts,
        (w_gate, w_out, w_attn_cond, line(b_attn_cond), line(gain_two), w_scale_two, line(b_scale_two), w_shift_two,
         w_hidden_gate, w_hidden_up, w_hidden_down, w_tr_cond, line(b_tr_cond)),
    )

    shape = (samples, rows, wide)
    d_x = None
    bias_grads, w_grads, q_grads = [], [], []
    for k, (own, sent) in enumerate(((da0, da1), (da2, da3))):
        out, probs, q, key, value, total = kept[k]
        d_x, db, gw, gb = attend_back(
            meta, blocks, w_heads[k], probs, q, key, value, total, out, own.reshape(shape), swap(sent, 1).reshape(shape),
            d_x, chunks, complexes, nh=few, hd=dim)
        bias_grads.append(lax.psum_scatter(ungroup(db), "samp", scatter_dimension=0, tiled=False))
        w_grads.append(gw)
        q_grads.append(gb)

    near = swap(jnp.stack([d_x[3], d_x[1]]), 1)
    far = swap(d_x[2] + near[0], 2)
    flat = lambda v: v.reshape(tokens, width)
    grad_single, g_scale1, g_shift1, s_scale1, s_gain1 = last(
        (flat(d_x[0]), flat(near[1]), flat(far), d_xg), single_t, cond_t, d_mid,
        line(gain_one), w_scale_one, line(b_scale_one), w_shift_one,
    )

    db = jnp.stack(bias_grads, axis=1)
    own, sent = db[..., :rows], db[..., rows:]
    other = swap(sent, 1)
    first = core == 0
    db = jnp.stack([jnp.where(first, own, other), jnp.where(first, other, own)], axis=2)
    db = db.reshape(complexes, heads, columns, rows)
    grad_pair_weight = jnp.einsum("cijz,chji->zh", pair_low, db, preferred_element_type=f32)
    d_pair_norm = jnp.einsum("chji,zh->cijz", db, w_pair, preferred_element_type=f32)
    grad_pair = norm_back(pair_normed, pair_inverse, d_pair_norm)

    def total(stack):
        part_sum = lax.psum_scatter(stack.astype(bf16), "head", scatter_dimension=2, tiled=True).astype(f32)
        return lax.psum_scatter(part_sum, "samp", scatter_dimension=0, tiled=True)

    r_down = total(g_dn[:, None])
    r_hidden = total(jnp.stack([g_hg, g_hu], axis=1))
    r_square = total(jnp.stack([g_out, g_gate], axis=1))
    r_cond = total(jnp.stack([g_tc, g_ac, g_scale2, g_shift2], axis=1))
    r_cond1 = total(jnp.stack([g_scale1, g_shift1], axis=1))
    keep = jnp.where(part == 0, w_grads[0], w_grads[1])
    send = jnp.where(part == 0, w_grads[1], w_grads[0])
    r_heads = keep + swap(send.astype(bf16), 2).astype(f32)
    r_heads = lax.psum_scatter(r_heads.T, "samp", scatter_dimension=0, tiled=True)

    q_full = jnp.zeros((groups, wide), f32)
    for k in range(groups // 2):
        q_full = lax.dynamic_update_index_in_dim(q_full, q_grads[k][:, 0], 2 * k + core, 0)
    column_sum = lambda v: jnp.sum(v, axis=0)
    small = lax.psum(
        (
            grad_pair_weight,
            column_sum(s_gain1),
            column_sum(s_gain2),
            column_sum(s_scale1),
            q_full.reshape(-1),
            column_sum(s_ac),
            column_sum(s_scale2),
            column_sum(s_tc),
        ),
        ("samp", "head"),
    )
    whole = (samples, rows, width)
    return (
        block_out.reshape(whole),
        grad_single.reshape(whole),
        grad_pair,
        small[1],
        r_cond1[:, 0],
        small[3],
        r_cond1[:, 1],
        r_heads[:, :wide],
        small[4],
        r_heads[:, wide : 2 * wide],
        r_heads[:, 2 * wide :],
        r_square[:, 1],
        r_square[:, 0],
        small[0],
        r_cond[:, 1],
        small[5],
        small[2],
        r_cond[:, 2],
        small[6],
        r_cond[:, 3],
        r_hidden[:, 0],
        r_hidden[:, 1],
        r_down[:, 0],
        r_cond[:, 0],
        small[7],
    )


def solution(mesh):
    placed = (
        P("samp", "head", None),
        P("samp", "head", None),
        P(None, "head", "samp", None),
        P(),
        P("samp"),
        P("samp", "head", None),
        P(),
        P(),
        P(),
        P(),
        P(),
        P(),
        P(),
        P(),
        P(),
        P(),
        P(),
        P(),
        P(),
        P(),
        P(),
        P(),
        P(),
        P(),
        P(),
        P(),
        P(),
        P(),
    )
    return jax.shard_map(
        on_device,
        mesh=mesh,
        in_specs=placed,
        out_specs=(
            P("samp", "head", None),
            P("samp", "head", None),
            P(None, "head", "samp", None),
            P(),
            P("samp", "head"),
            P(),
            P("samp", "head"),
            P("samp", "head"),
            P(),
            P("samp", "head"),
            P("samp", "head"),
            P("samp", "head"),
            P("samp", "head"),
            P(),
            P("samp", "head"),
            P(),
            P(),
            P("samp", "head"),
            P(),
            P("samp", "head"),
            P("samp", "head"),
            P("samp", "head"),
            P("samp", "head"),
            P("samp", "head"),
            P(),
        ),
        check_vma=False,
    )
```

time: 2600 us -> 1330 us (0.51)
  blocking collectives: 815 us -> 41.4 us
  matrix products: 428 us -> 54.6 us
  local copies, waits for them, and re-layouts: 526 us -> 250 us
  Pallas kernels: 0 us -> 263 us
  other arithmetic: 214 us -> 93.2 us
  waiting for transfers between devices: 514 us -> 597 us
  starting transfers between devices: 42.6 us -> 8.41 us
  loops' own time: 32.8 us -> 0 us
    unnamed x1 -> x0, blocking collectives: 752 us -> none
    dot_general x99 -> x3, matrix products: 428 us -> 54.6 us  [the longest x1 34.5 us: on_device(): jnp.einsum('chji,zh->cijz', db, w_pair, preferred_element_type=f32)]
    pallas_call x0 -> x7, Pallas kernels: none -> 263 us  [the longest x2 93.2 us: attend_back(): pl.pallas_call(kern, grid_spec=pltpu.PrefetchScalarGridSpec(num_scalar_pr...]
    all_to_all x9 -> x0, waiting for transfers between devices: 199 us -> none  [the longest x1 33.5 us: on_device(): lax.all_to_all(d_attended, 'head', split_axis=2, concat_axis=1, tiled=True)]
    unnamed x189 -> x121, local copies, waits for them, and re-layouts: 42.5 us -> 192 us
    dynamic_slice x88 -> x6, local copies, waits for them, and re-layouts: 149 us -> 4.6 us  [the longest x3 3.72 us: own_columns(): return lax.dynamic_slice_in_dim(w, (2 * k + core) * wide, wide, w.ndim - 1)]
    dynamic_update_slice x32 -> x2, local copies, waits for them, and re-layouts: 127 us -> 0.08 us  [on_device(): lax.dynamic_update_index_in_dim(q_full, q_grads[k][:, 0], 2 * k + core, 0)]
    ppermute x0 -> x12, waiting for transfers between devices: none -> 126 us  [swap(): return lax.ppermute(value, 'head', [(i, i ^ bit) for i in range(size)])]
  transfers between devices with their start and end apart: 38 -> 24, of which waited for: 17 -> 16; matrix products, arithmetic and copies ran while one was open for 32% -> 25% of each run, Pallas kernels for 0% -> 9%
where the time goes in v1:
time: 1330 us; the launch traced here: 1320 us
  waiting for transfers between devices  597 us (45%)
  Pallas kernels  263 us (20%)
  local copies, waits for them, and re-layouts  250 us (19%)
  other arithmetic  93.2 us (7%)
  matrix products  54.6 us (4%)
  blocking collectives  41.4 us (3%)
  between operations  16.8 us (1%)
    unnamed x121, local copies, waits for them, and re-layouts  192 us
    unnamed x18, waiting for transfers between devices  172 us
    reduce_scatter x2, waiting for transfers between devices, on_device(): lax.psum_scatter(ungroup(db), 'samp', scatter_dimension=0, tiled=False)  146 us
    ppermute x12, waiting for transfers between devices, swap(): return lax.ppermute(value, 'head', [(i, i ^ bit) for i in range(size)])  126 us
    reduce_scatter x2, waiting for transfers between devices, total(): return lax.psum_scatter(part_sum, 'samp', scatter_dimension=0, tiled=True)  97.5 us
    pallas_call x2, Pallas kernels, attend_back(): pl.pallas_call(kern, grid_spec=pltpu.PrefetchScalarGridSpec(num_scalar_pr...  93.2 us
    pallas_call x1, Pallas kernels, middle(): pl.pallas_call(middle_kernel, grid_spec=pltpu.PrefetchScalarGridSpec(num_...  83.3 us
    pallas_call x2, Pallas kernels, attend(): pl.pallas_call(kern, grid_spec=pltpu.PrefetchScalarGridSpec(num_scalar_pr...  63.3 us
  transfers between devices with their start and end apart: 24, of which 16 were waited for; matrix products, arithmetic and copies ran while one was open for 25% of the time, Pallas kernels for 9%

profile of v1, /device:TPU:0, one launch (start us, length us, event | category | flops | bytes accessed | tf_op | source)
XLA Modules:
  0.0 1324.4 jit_solution(3744146639158313637)
XLA Ops:
  64.9 51.8 %collective-permute-done.1 = bf16[1536,768]{1,0:T(8,128)(2,1)} collective-permute-done((bf16[1536,768]{1,0:T(8,128)(2,1)}, bf16[1536,768]{1,0:T(8,128)(2,1)}, u32[]{:S(2)}, u32[]{:S(2)}) %collective-permute-start.1) | collective-permute-done | bytes 2359328 | tf_op jit(solution)/shard_map/ppermute | solution.py:390
  134.4 31.7 %attend.3 = (bf16[2,8,192,192]{3,2,1,0:T(8,128)(2,1)}, bf16[8,4,768,384]{3,2,1,0:T(8,128)(2,1)}, bf16[8,192,384]{2,1,0:T(8,128)(2,1)}, bf16[8,192,768]{2,1,0:T(8...) custom-call(s32[9]{0:T(128)} %pad_add_fusion.meta, bf16[8,192,768]{2,1,0:T(8,128)(2,1)} %bitcast.162, ...), custom_call_target="tpu_custom_call" | custom-call | flops 30000001024 | bytes 60000000 | tf_op jit(solution)/shard_map/attend/pallas_call | solution.py:90
  168.5 46.7 %all-gather.5.cloned.1.call-done = bf16[16,1,4,96,384]{4,3,2,1,0:T(8,128)(2,1)} async-done(((bf16[2,1,4,96,384]{4,3,2,1,0:T(8,128)(2,1)}), bf16[16,1,4,96,384]{4,3,2,1,0:T(8,128)(2,1)}) %all-gather.5.cloned.1.call-update) | async-done | bytes 4718608 | tf_op jit(solution)/shard_map/all_gather | solution.py:463
  215.2 31.6 %attend.2 = (bf16[2,8,192,192]{3,2,1,0:T(8,128)(2,1)}, bf16[8,4,768,384]{3,2,1,0:T(8,128)(2,1)}, bf16[8,192,384]{2,1,0:T(8,128)(2,1)}, bf16[8,192,768]{2,1,0:T(8...) custom-call(s32[9]{0:T(128)} %pad_add_fusion.meta, bf16[8,192,768]{2,1,0:T(8,128)(2,1)} %bitcast.163, ...), custom_call_target="tpu_custom_call" | custom-call | flops 30000001024 | bytes 60000000 | tf_op jit(solution)/shard_map/attend/pallas_call | solution.py:90
  252.8 83.3 %middle.1 = (bf16[1536,768]{1,0:T(8,128)(2,1)}, f32[1536,768]{1,0:T(8,128)}, bf16[1536,768]{1,0:T(8,128)(2,1)}, bf16[1536,192]{1,0:T(8,128)(2,1)}, bf16[1536,192...) custom-call(s32[9]{0:T(128)} %pad_add_fusion.meta, ...), custom_call_target="tpu_custom_call" | custom-call | flops 54358179840 | bytes 62914560 | tf_op jit(solution)/shard_map/middle/pallas_call | solution.py:329
  340.9 46.2 %attend_back.2 = (bf16[4,8,192,768]{3,2,1,0:T(8,128)(2,1)}, bf16[8,2,4,96,384]{4,3,2,1,0:T(8,128)(2,1)}, f32[576,768]{1,0:T(8,128)}, f32[192,1]{1,0:T(8,128)}) custom-call(s32[9]{0:T(128)} %pad_add_fusion.meta, bf16[8,192,768]{2,1,0:T(8,128)(2,1)} %bitcast.164, bf16[8,192,768]{2,1,0:T(8,128)(2,1)} %bitcast.5.x1, bf16[8,192,768]{2,1,0:T(8,128)(2,1)} %bitcast.6.x2, ...), custom_call_target="tpu_custom_call" | custom-call | flops 60000002048 | bytes 60000000 | tf_op jit(solution)/shard_map/attend_back/pallas_call | solution.py:179
  388.3 47.0 %attend_back.3 = (bf16[4,8,192,768]{3,2,1,0:T(8,128)(2,1)}, bf16[8,2,4,96,384]{4,3,2,1,0:T(8,128)(2,1)}, f32[576,768]{1,0:T(8,128)}, f32[192,1]{1,0:T(8,128)}) custom-call(s32[9]{0:T(128)} %pad_add_fusion.meta, bf16[8,192,768]{2,1,0:T(8,128)(2,1)} %bitcast.165, bf16[8,192,768]{2,1,0:T(8,128)(2,1)} %bitcast.5.x1, bf16[8,192,768]{2,1,0:T(8,128)(2,1)} %bitcast.6.x2, ...), custom_call_target="tpu_custom_call" | custom-call | flops 60000002048 | bytes 60000000 | tf_op jit(solution)/shard_map/attend_back/pallas_call | solution.py:179
  463.7 40.0 %collective-permute-done.9 = bf16[8,192,768]{2,1,0:T(8,128)(2,1)} collective-permute-done((bf16[8,192,768]{2,1,0:T(8,128)(2,1)}, bf16[8,192,768]{2,1,0:T(8,128)(2,1)}, u32[]{:S(2)}, u32[]{:S(2)}) %collective-permute-start.9) | collective-permute-done | bytes 2359328 | tf_op jit(solution)/shard_map/ppermute | solution.py:390
  503.7 15.5 %last.1 = (f32[1536,768]{1,0:T(8,128)}, f32[384,768]{1,0:T(8,128)}, f32[384,768]{1,0:T(8,128)}, f32[8,768]{1,0:T(8,128)}, f32[8,384]{1,0:T(8,128)}) custom-call(bf16[1536,768]{1,0:T(8,128)(2,1)} %bitcast.166, bf16[1536,768]{1,0:T(8,128)(2,1)} %bitcast.167, bf16[1536,768]{1,0:T(8,128)(2,1)} %bitcast.37.d2, bf16[1536,768]{1,0:T(8,128)(2,1)} %get-tuple-element.89.d3, ...), custom_call_target="tpu_custom_call" | custom-call | flops 5435817984 | bytes 31457280 | tf_op jit(solution)/shard_map/last/pallas_call | solution.py:374
  571.1 24.9 %collective-permute-done.11 = bf16[576,768]{1,0:T(8,128)(2,1)S(1)} collective-permute-done((bf16[576,768]{1,0:T(8,128)(2,1)S(1)}, bf16[576,768]{1,0:T(8,128)(2,1)S(1)}, u32[]{:S(2)}, u32[]{:S(2)}) %collective-permute-start.11) | collective-permute-done | bytes 884768 | tf_op jit(solution)/shard_map/ppermute | solution.py:390
  599.6 44.4 %all-reduce.13.cloned.1.call-done = (bf16[384,2,768]{0,1,2:T(2,128)(2,1)}, bf16[384,4,768]{0,1,2:T(4,128)(2,1)}, bf16[768,2,768]{0,1,2:T(2,128)(2,1)}) async-done(((bf16[384,2,768]{0,1,2:T(2,128)(2,1)}, bf16[384,4,768]{0,1,2:T(4,128)(2,1)}, bf16[768,2,768]{0,1,2:T(2,128)(2,1)}), (bf16[384,2,768]{0,1,2:T(2,128)(2,1)}, bf16[384,4,768]{0,1,2:T(4,128)(2,1)}, ...) | async-done | bytes 5898256
  651.0 37.0 %copy.186 = f32[768,2,192]{1,2,0:T(8,128)} copy(f32[768,2,192]{0,1,2:T(2,128)S(1)} %dynamic-slice_convert_fusion) | data formatting | bytes 2359296
  688.0 52.6 %reshape.212 = f32[768,384]{1,0:T(8,128)} reshape(f32[768,192,2]{2,1,0:T(8,128)} %bitcast.67) | data formatting | bytes 2359296
  747.3 46.9 %reduce-scatter.19.cloned.1.call-done = bf16[1,2,4,96,384]{4,3,2,1,0:T(8,128)(2,1)} async-done(((bf16[8,2,4,96,384]{4,3,2,1,0:T(8,128)(2,1)}), bf16[1,2,4,96,384]{4,3,2,1,0:T(8,128)(2,1)}) %reduce-scatter.19.cloned.1.call-update) | async-done | bytes 589840 | tf_op jit(solution)/shard_map/reduce_scatter | solution.py:507
  794.2 99.0 %reduce-scatter.17.cloned.1.call-done = bf16[1,2,4,96,384]{4,3,2,1,0:T(8,128)(2,1)} async-done(((bf16[8,2,4,96,384]{4,3,2,1,0:T(8,128)(2,1)}), bf16[1,2,4,96,384]{4,3,2,1,0:T(8,128)(2,1)}) %reduce-scatter.17.cloned.1.call-update) | async-done | bytes 589840 | tf_op jit(solution)/shard_map/reduce_scatter | solution.py:507
  910.2 18.5 %reduce-scatter.31.cloned.1.call-done = bf16[192,1536]{1,0:T(8,128)(2,1)} async-done(((bf16[768,1536]{1,0:T(8,128)(2,1)}), bf16[192,1536]{1,0:T(8,128)(2,1)}) %reduce-scatter.31.cloned.1.call-update) | async-done | bytes 589840
  932.7 66.3 %reduce-scatter.25.cloned.1.call-done = f32[96,576]{1,0:T(8,128)} async-done(((f32[768,576]{1,0:T(8,128)}), f32[96,576]{1,0:T(8,128)}) %reduce-scatter.25.cloned.1.call-update) | async-done | bytes 221200
  1002.6 34.5 %bitcast_reduce_fusion = (f32[2,192,96]{1,2,0:T(8,128)S(1)}, f32[2,192,96]{1,2,0:T(8,128)S(1)}, f32[2,96,192,128]{3,2,1,0:T(8,128)}) fusion(f32[2,192,96]{1,2,0:T(8,128)S(1)} %copy-done.10, f32[2,192,96]{1,2,0:T(8,128)S(1)} %copy-done.5, bf16[2,192,96,128]{3,2,1,0:T(8,128)(2,1)} %param.30, bf16[128,16]{0,1:T(8,128)(2,1)S(1)} %copy-done, ...), kind=kOutput, calls=%fused_computation.12 | convolution fusion | flops 179232768 | bytes 30085120 | tf_op jit(solution)/shard_map/chji,zh->cijz/dot_general | solution.py:526
  1037.1 23.3 %fusion.7 = f32[2,192,96,128]{3,1,2,0:T(8,128)S(1)} fusion(f32[2,96,192,128]{3,2,1,0:T(8,128)} %get-tuple-element.291, f32[2,192,96]{1,2,0:T(8,128)S(1)} %broadcast_multiply_fusion, f32[2,192,96]{1,2,0:T(8,128)S(1)} %broadcast_multiply_fusion.1, f32[2,192,96]{1,2,0:T(8,128)S(1)} %copy-done.10, f32[2,192,96]{1,2,0:T(8,128)S(1)} %copy-done.5, ...), kind=kLoop, calls=%fused_computation.9 | loop fusion | flops 33030144 | bytes 47775744 | tf_op jit(solution)/shard_map/mul | solution.py:34
  1060.5 22.9 %copy.176 = f32[2,192,96,128]{3,2,1,0:T(8,128)} copy(f32[2,192,96,128]{3,1,2,0:T(8,128)S(1)} %fusion.7) | data formatting | bytes 37748736
  1089.4 41.4 %all-reduce.5 = (f32[384]{0:T(512)}, f32[768]{0:T(1024)}, f32[768]{0:T(1024)}, f32[128,16]{0,1:T(8,128)}, f32[768]{0:T(1024)}, /*index=5*/f32[384]{0:T(512)}, f32[768]{0:T(1024)}, f32[768]{0:T(1024)}) all-reduce(f32[384]{0:T(512)S(1)} %reduce_sum.94, f32[768]{0:T(1024)S(1)} %reduce_sum.95, ...), channel_id=1, replica_groups=mesh['samp'=8,'head'=4] {'samp','head'}, use_global_device_ids=true, to_apply=%region_7.8 | all-reduce | flops 6656 | bytes 53248 | tf_op jit(solution)/shard_map/psum | solution.py:547
  1137.1 40.9 %reduce-scatter.27.cloned.1.call-done = f32[96,384]{1,0:T(8,128)} async-done(((f32[768,384]{1,0:T(8,128)}), f32[96,384]{1,0:T(8,128)}) %reduce-scatter.27.cloned.1.call-update) | async-done | bytes 147472
  1218.1 31.4 %reduce-scatter.21.cloned.1.call-done = f32[96,2,384]{2,0,1:T(8,128)} async-done(((f32[768,2,384]{2,0,1:T(8,128)}), f32[96,2,384]{2,0,1:T(8,128)}) %reduce-scatter.21.cloned.1.call-update) | async-done | bytes 294928 | tf_op jit(solution)/shard_map/reduce_scatter | solution.py:531
  1251.2 66.1 %reduce-scatter.23.cloned.1.call-done = f32[192,1,192]{2,0,1:T(8,128)} async-done(((f32[1536,1,192]{2,0,1:T(8,128)}), f32[192,1,192]{2,0,1:T(8,128)}) %reduce-scatter.23.cloned.1.call-update) | async-done | bytes 147472 | tf_op jit(solution)/shard_map/reduce_scatter | solution.py:531
  (256 shorter events, 263.7 us)
Async XLA Ops:
  7.2 127.1 %all-gather.7.cloned.1.call-start = ((), (), s32[]{:S(2)}) async-start(), calls=%async_computation.13 | async-start | bytes 5308416 | tf_op jit(solution)/shard_map/all_gather | solution.py:463
  47.8 2.4 collective-permute-start.3
  51.7 163.5 %all-gather.5.cloned.1.call-start = ((), (), s32[]{:S(2)}) async-start(), calls=%async_computation.12 | async-start | bytes 5308416 | tf_op jit(solution)/shard_map/all_gather | solution.py:463
  52.5 591.6 %all-reduce.13.cloned.1.call-start = ((), (), s32[]{:S(2)}) async-start(), calls=%async_computation.19 | async-start | bytes 11796480
  62.0 54.8 %collective-permute-start.1 = (bf16[1536,768]{1,0:T(8,128)(2,1)}, bf16[1536,768]{1,0:T(8,128)(2,1)}, u32[]{:S(2)}, u32[]{:S(2)}) collective-permute-start(bf16[1536,768]{1,0:T(8,128)(2,1)} %adapt.1.x_ref), channel_id=1, source_target_pairs={{0,2},{1,3},{2,0},{3,1},{4,6},{5,7},{6,4},{7,5},{8,10},{9,11},{10,... | collective-permute-start | bytes 7077896 | tf_op jit(solution)/shard_map/ppermute | solution.py:390
  64.9 60.7 %collective-permute-start = (bf16[1536,768]{1,0:T(8,128)(2,1)}, bf16[1536,768]{1,0:T(8,128)(2,1)}, u32[]{:S(2)}, u32[]{:S(2)}) collective-permute-start(bf16[1536,768]{1,0:T(8,128)(2,1)} %adapt.1.x_ref), channel_id=1, source_target_pairs={{0,1},{1,0},{2,3},{3,2},{4,5},{5,4},{6,7},{7,6},{8,9},{9,8},{10,11... | collective-permute-start | bytes 7077896 | tf_op jit(solution)/shard_map/ppermute | solution.py:390
  116.8 8.8 collective-permute-start.2
  168.4 83.2 %collective-permute-start.5 = (bf16[8,192,192]{2,1,0:T(8,128)(2,1)S(1)}, bf16[8,192,192]{2,1,0:T(8,128)(2,1)S(1)}, u32[]{:S(2)}, u32[]{:S(2)}) collective-permute-start(bf16[8,192,192]{2,1,0:T(8,128)(2,1)S(1)} %get-tuple-element.268), channel_id=1, source_target_pairs={{0,1},{1,0},{2,3},{3,2},{4,5},{5,4},{6,7},{7,6},{8,9},{9,8},{10,11... | collective-permute-start | bytes 1769480 | tf_op jit(solution)/shard_map/ppermute | solution.py:390
  249.3 2.3 collective-permute-start.4
  337.6 2.2 collective-permute-start.7
  339.5 47.6 %collective-permute-start.6 = (bf16[1536,192]{0,1:T(8,128)(2,1)S(1)}, bf16[1536,192]{0,1:T(8,128)(2,1)S(1)}, u32[]{:S(2)}, u32[]{:S(2)}) collective-permute-start(bf16[1536,192]{0,1:T(8,128)(2,1)S(1)} %copy.162), channel_id=1, source_target_pairs={{0,1},{1,0},{2,3},{3,2},{4,5},{5,4},{6,7},{7,6},{8,9},{9,8},{10,11... | collective-permute-start | bytes 1769480 | tf_op jit(solution)/shard_map/ppermute | solution.py:390
  438.8 8.0 collective-permute-start.8
  449.8 53.8 %collective-permute-start.9 = (bf16[8,192,768]{2,1,0:T(8,128)(2,1)}, bf16[8,192,768]{2,1,0:T(8,128)(2,1)}, u32[]{:S(2)}, u32[]{:S(2)}) collective-permute-start(bf16[8,192,768]{2,1,0:T(8,128)(2,1)} %get-tuple-element.257), channel_id=1, source_target_pairs={{0,2},{1,3},{2,0},{3,1},{4,6},{5,7},{6,4},{7,5},{8,10},{9,11},{10,... | collective-permute-start | bytes 7077896 | tf_op jit(solution)/shard_map/ppermute | solution.py:390
  523.9 216.8 %reduce-scatter.29.cloned.1.call-start = ((), (), s32[]{:S(2)}) async-start(), calls=%async_computation.16 | async-start | bytes 5898240
  550.9 243.3 %reduce-scatter.19.cloned.1.call-start = ((), (), s32[]{:S(2)}) async-start(), calls=%async_computation.9 | async-start | bytes 5308416 | tf_op jit(solution)/shard_map/reduce_scatter | solution.py:507
  551.5 341.7 %reduce-scatter.17.cloned.1.call-start = ((), (), s32[]{:S(2)}) async-start(), calls=%async_computation.8 | async-start | bytes 5308416 | tf_op jit(solution)/shard_map/reduce_scatter | solution.py:507
  552.0 376.7 %reduce-scatter.31.cloned.1.call-start = ((), (), s32[]{:S(2)}) async-start(), calls=%async_computation.17 | async-start | bytes 2949120
  567.8 431.2 %reduce-scatter.25.cloned.1.call-start = ((), (), s32[]{:S(2)}) async-start(), calls=%async_computation.14 | async-start | bytes 2211840
  569.5 26.5 %collective-permute-start.11 = (bf16[576,768]{1,0:T(8,128)(2,1)S(1)}, bf16[576,768]{1,0:T(8,128)(2,1)S(1)}, u32[]{:S(2)}, u32[]{:S(2)}) collective-permute-start(bf16[576,768]{1,0:T(8,128)(2,1)S(1)} %select_convert_fusion.1), channel_id=1, source_target_pairs={{0,2},{1,3},{2,0},{3,1},{4,6},{5,7},{6,4},{7,5},{8,10},{9,11},{10,... | collective-permute-start | bytes 2654216 | tf_op jit(solution)/shard_map/ppermute | solution.py:390
  598.3 532.5 %all-reduce.11.cloned.1.call-start = ((), (), s32[]{:S(2)}) async-start(), calls=%async_computation.18 | async-start | bytes 4718592
  649.5 528.4 %reduce-scatter.27.cloned.1.call-start = ((), (), s32[]{:S(2)}) async-start(), calls=%async_computation.15 | async-start | bytes 1327104
  740.6 508.9 %reduce-scatter.21.cloned.1.call-start = ((), (), s32[]{:S(2)}) async-start(), calls=%async_computation.10 | async-start | bytes 2654208 | tf_op jit(solution)/shard_map/reduce_scatter | solution.py:531
  747.2 570.2 %reduce-scatter.23.cloned.1.call-start = ((), (), s32[]{:S(2)}) async-start(), calls=%async_computation.11 | async-start | bytes 1769472 | tf_op jit(solution)/shard_map/reduce_scatter | solution.py:531
  894.7 106.1 %collective-permute-start.10 = (bf16[2,2,4,96,192]{4,3,2,0,1:T(8,128)(2,1)S(1)}, bf16[2,2,4,96,192]{4,3,2,0,1:T(8,128)(2,1)}, u32[]{:S(2)}, u32[]{:S(2)}) collective-permute-start(bf16[2,2,4,96,192]{4,3,2,0,1:T(8,128)(2,1)S(1)} %pad_maximum_fusion.8), channel_id=1, source_target_pairs={{0,1},{1,0},{2,3},{3,2},{4,5},{5,4},{6,7},{7,6},{8,9},{9,8},{10,11... | collective-permute-start | bytes 1769480 | tf_op jit(solution)/shard_map/ppermute | solution.py:390
  (44 other events, 1020.4 us)
Sparse Core Ops, SparseCore 0:
  51.8 82.4 all-gather.6
  137.1 78.0 all-gather.4
  524.0 119.9 all-reduce.12
  647.0 47.9 reduce-scatter.28
  698.9 95.2 reduce-scatter.18
  798.1 95.0 reduce-scatter.16
  895.9 32.8 reduce-scatter.30
  932.2 66.7 reduce-scatter.24
  1003.1 108.4 all-reduce.10
  1114.8 63.0 reduce-scatter.26
  1181.4 68.0 reduce-scatter.20
  1253.4 63.9 reduce-scatter.22
